TPU v7x, 32 devices: a whole 2x2x4 slice. The times are simulated.
32 devices in a mesh: zonal: 8 (over z, x), merid: 4 (over y, core).
Axes of the slice: x: 2, y: 2, z: 4, core: 2. Of those that a mesh axis runs over, the one named last changes fastest.
Arguments:
- field: bfloat16 [64, 512, 256], P('merid', 'zonal'), may hold values from -6 to 6
- weight_one: bfloat16 [3, 3, 256, 256], replicated, may hold values from -0.125 to 0.125
- bias_one: float32 [256], replicated, may hold values from -3 to 3
- weight_two: bfloat16 [3, 3, 256, 256], replicated, may hold values from -0.125 to 0.125
- bias_two: float32 [256], replicated, may hold values from -3 to 3
- depth_levels: int32 [64, 512], P('merid', 'zonal'), may hold values from 0 to 64
- fold_partner: int32 [512], replicated, may hold values from 0 to 511, as said below
- cotangent: bfloat16 [64, 512, 256], P('merid', 'zonal'), may hold values from -6 to 6
Outputs:
- output: bfloat16 [64, 512, 256], P('merid', 'zonal')
- input_grad: bfloat16 [64, 512, 256], P('merid', 'zonal')
- grad_one: float32 [3, 3, 256, 256], replicated
- grad_two: float32 [3, 3, 256, 256], replicated
Inputs may be any that keep to these rules, and one draw needn't show every extreme that they name: fold_partner[i] = (511 - i + s) mod 512 with one pivot offset s, 0 to 511, for the whole table.
All inputs are finite; a program needn't handle non-finite values.
Results may differ from a plain program's by a relative error of at most 0.003.
Values may be sent and summed in bfloat16 or wider, within the bound.
A program may use at most 128 MiB of HBM per device.

v0:
```python
import math

import jax
import jax.numpy as jnp
from jax import lax
from jax.sharding import PartitionSpec as P

LEV = 64


def with_halo(cells, sides, width, closed):
    for axis, dim in sides:
        count = lax.axis_size(axis)
        ends = count if closed else count - 1
        head = lax.slice_in_dim(cells, 0, width, axis=dim)
        tail = lax.slice_in_dim(cells, cells.shape[dim] - width, cells.shape[dim], axis=dim)
        cells = jnp.concatenate(
            [
                lax.ppermute(tail, axis, [(i, (i + 1) % count) for i in range(ends)]),
                cells,
                lax.ppermute(head, axis, [((i + 1) % count, i) for i in range(ends)]),
            ],
            axis=dim,
        )
    return cells


def level_mask(depth_levels, channels):
    level_index = lax.broadcasted_iota(jnp.int32, (1, 1, channels), 2) % LEV
    return (level_index < depth_levels[:, :, None]).astype(jnp.float32)


def fold_forward(top_row, fold_partner):
    columns = top_row.shape[0]
    whole_row = lax.all_gather(top_row, "zonal", axis=0, tiled=True)
    partners = lax.dynamic_slice_in_dim(fold_partner, lax.axis_index("zonal") * columns, columns, 0)
    return jnp.take(whole_row, partners, axis=0)


def fold_backward(fold_grad, fold_partner):
    columns = fold_grad.shape[0]
    whole_row = lax.all_gather(fold_grad.astype(jnp.bfloat16), "zonal", axis=0, tiled=True).astype(
        fold_grad.dtype
    )
    partners = lax.dynamic_slice_in_dim(fold_partner, lax.axis_index("zonal") * columns, columns, 0)
    return jnp.take(whole_row, partners, axis=0)


def pad_field(values, fold_partner, is_top):
    with_rows = with_halo(values, (("merid", 0),), 1, False)
    fold_row = fold_forward(values[-1], fold_partner)
    upper_row = jnp.where(is_top, fold_row, with_rows[-1])
    with_rows = jnp.concatenate([with_rows[:-1], upper_row[None]], axis=0)
    return with_halo(with_rows, (("zonal", 1),), 1, True)


def unpad_grad(grad_pad, fold_partner, is_top):
    sides = jnp.concatenate([grad_pad[:, :1], grad_pad[:, -1:]], axis=1)
    returned = with_halo(sides.astype(jnp.bfloat16), (("zonal", 1),), 1, True).astype(sides.dtype)
    inner = grad_pad[:, 1:-1]
    inner = inner.at[:, 0].add(returned[:, 0]).at[:, -1].add(returned[:, 3])
    rims = jnp.concatenate([inner[:1], inner[-1:]], axis=0)
    back_rows = with_halo(rims.astype(jnp.bfloat16), (("merid", 0),), 1, False).astype(rims.dtype)
    folded = fold_backward(inner[-1], fold_partner)
    top_added = back_rows[3] + jnp.where(is_top, folded, jnp.zeros_like(folded))
    middle = inner[1:-1]
    return middle.at[0].add(back_rows[0]).at[-1].add(top_added)


def patches_of(padded, rows, columns):
    pieces = [
        padded[row_step : row_step + rows, col_step : col_step + columns]
        for row_step in range(3)
        for col_step in range(3)
    ]
    return jnp.concatenate(pieces, axis=2).reshape(rows * columns, -1)


def transpose_conv(delta, flat_weight, rows, columns):
    channels = delta.shape[1]
    parts = lax.dot_general(
        delta, flat_weight, (((1,), (1,)), ((), ())), preferred_element_type=jnp.float32
    )
    parts = parts.reshape(rows, columns, 9, channels)
    grad_pad = jnp.zeros((rows + 2, columns + 2, channels), jnp.float32)
    for row_step in range(3):
        for col_step in range(3):
            grad_pad = grad_pad.at[row_step : row_step + rows, col_step : col_step + columns].add(
                parts[:, :, 3 * row_step + col_step]
            )
    return grad_pad


def kernel_grad(patches, delta):
    channels = delta.shape[1]
    summed = lax.dot_general(
        patches, delta, (((0,), (0,)), ((), ())), preferred_element_type=jnp.float32
    )
    return summed.reshape(3, 3, channels, channels)


def shards(
    field, weight_one, bias_one, weight_two, bias_two, depth_levels, fold_partner, cotangent
):
    rows, columns, channels = field.shape
    is_top = lax.axis_index("merid") == lax.axis_size("merid") - 1
    mask = level_mask(depth_levels, channels)
    flat_one = weight_one.reshape(9 * channels, channels)
    flat_two = weight_two.reshape(9 * channels, channels)
    patches_one = patches_of(pad_field(field, fold_partner, is_top), rows, columns)
    pre_one = (
        jnp.dot(patches_one, flat_one, preferred_element_type=jnp.float32).reshape(
            rows, columns, channels
        )
        + bias_one
    )
    hidden = (jax.nn.gelu(pre_one) * mask).astype(jnp.bfloat16)
    patches_two = patches_of(pad_field(hidden, fold_partner, is_top), rows, columns)
    pre_two = jnp.dot(patches_two, flat_two, preferred_element_type=jnp.float32).reshape(
        rows, columns, channels
    )
    output = ((field.astype(jnp.float32) + pre_two + bias_two) * mask).astype(jnp.bfloat16)
    masked_grad = cotangent.astype(jnp.float32) * mask
    delta_two = masked_grad.astype(jnp.bfloat16).reshape(rows * columns, channels)
    grad_two = kernel_grad(patches_two, delta_two)
    hidden_grad = unpad_grad(
        transpose_conv(delta_two, flat_two, rows, columns), fold_partner, is_top
    )
    _, gelu_back = jax.vjp(jax.nn.gelu, pre_one)
    delta_one = (
        gelu_back(hidden_grad * mask)[0].astype(jnp.bfloat16).reshape(rows * columns, channels)
    )
    grad_one = kernel_grad(patches_one, delta_one)
    field_grad = unpad_grad(
        transpose_conv(delta_one, flat_one, rows, columns), fold_partner, is_top
    )
    input_grad = (masked_grad + field_grad).astype(jnp.bfloat16)
    grad_one, grad_two = lax.psum((grad_one, grad_two), ("zonal", "merid"))
    scale = 1.0 / math.sqrt(rows * columns * lax.axis_size("zonal") * lax.axis_size("merid"))
    return (output, input_grad, grad_one * scale, grad_two * scale)


def solution(mesh):
    placed = (
        P("merid", "zonal", None),
        P(),
        P(),
        P(),
        P(),
        P("merid", "zonal"),
        P(),
        P("merid", "zonal", None),
    )
    return jax.shard_map(
        shards,
        mesh=mesh,
        in_specs=placed,
        out_specs=(P("merid", "zonal", None), P("merid", "zonal", None), P(), P()),
        check_vma=False,
    )
```

profile of v0, /device:TPU:5, one launch (start us, length us, event | category | flops | bytes accessed | tf_op | source)
XLA Modules:
  0.0 431.9 jit_solution(333514012501296329)
XLA Ops:
  7.2 1.5 fusion.52
  8.7 3.2 collective-permute-start.1
  11.9 1.3 collective-permute-start
  14.5 2.9 fusion.35
  19.5 2.4 fusion.27
  22.6 6.4 %scatter-add.89 = f32[18,66,256]{2,1,0:T(8,128)S(1)} dynamic-update-slice(f32[18,66,256]{2,1,0:T(8,128)S(1)} %scatter-add.86, f32[16,64,256]{2,1,0:T(8,128)} %fusion.27, s32[]{:T(128)} %bitcast.15, s32[]{:T(128)} %bitcast.16, s32[]{:T(128)} %constant.689.clone.1) | dynamic-update-slice | bytes 2097156 | tf_op jit(solution)/shard_map/scatter-add | solution.py:88
  29.0 4.2 add_select_fusion.1
  33.2 6.4 %scatter-add.90 = f32[18,66,256]{2,1,0:T(8,128)S(1)} dynamic-update-slice(f32[18,66,256]{2,1,0:T(8,128)S(1)} %scatter-add.89, f32[16,64,256]{2,1,0:T(8,128)} %add_select_fusion.1, s32[]{:T(128)} %bitcast.18, s32[]{:T(128)} %bitcast.19, s32[]{:T(128)} %constant.689.clone.1) | dynamic-update-slice | bytes 2097156 | tf_op jit(solution)/shard_map/scatter-add | solution.py:88
  39.6 1.4 fusion.26
  41.1 2.4 fusion.24
  43.4 5.1 %scatter-add.94 = f32[18,66,256]{2,1,0:T(8,128)S(1)} dynamic-update-slice(f32[18,66,256]{2,1,0:T(8,128)S(1)} %fusion.26, f32[16,64,256]{2,1,0:T(8,128)} %fusion.24, s32[]{:T(128)} %constant.705.clone.1, s32[]{:T(128)} %constant.705.clone.1, s32[]{:T(128)} %constant.689.clone.1) | dynamic-update-slice | bytes 2097156 | tf_op jit(solution)/shard_map/scatter-add | solution.py:88
  48.5 2.4 fusion.23
  50.9 5.1 %scatter-add.95 = f32[18,66,256]{2,1,0:T(8,128)S(1)} dynamic-update-slice(f32[18,66,256]{2,1,0:T(8,128)S(1)} %scatter-add.94, f32[16,64,256]{2,1,0:T(8,128)} %fusion.23, s32[]{:T(128)} %constant.705.clone.1, s32[]{:T(128)} %constant.701.clone.1, s32[]{:T(128)} %constant.689.clone.1) | dynamic-update-slice | bytes 2097156 | tf_op jit(solution)/shard_map/scatter-add | solution.py:88
  56.0 1.4 fusion.22
  57.5 2.4 fusion.20
  59.9 5.1 %scatter-add.99 = f32[18,66,256]{2,1,0:T(8,128)S(1)} dynamic-update-slice(f32[18,66,256]{2,1,0:T(8,128)S(1)} %fusion.22, f32[16,64,256]{2,1,0:T(8,128)} %fusion.20, s32[]{:T(128)} %constant.701.clone.1, s32[]{:T(128)} %constant.705.clone.1, s32[]{:T(128)} %constant.689.clone.1) | dynamic-update-slice | bytes 2097156 | tf_op jit(solution)/shard_map/scatter-add | solution.py:88
  65.0 2.4 fusion.19
  67.3 5.1 %scatter-add.100 = f32[18,66,256]{2,1,0:T(8,128)S(1)} dynamic-update-slice(f32[18,66,256]{2,1,0:T(8,128)S(1)} %scatter-add.99, f32[16,64,256]{2,1,0:T(8,128)} %fusion.19, s32[]{:T(128)} %constant.701.clone.1, s32[]{:T(128)} %constant.701.clone.1, s32[]{:T(128)} %constant.689.clone.1) | dynamic-update-slice | bytes 2097156 | tf_op jit(solution)/shard_map/scatter-add | solution.py:88
  72.6 1.3 collective-permute-start.8
  73.9 3.1 collective-permute-start.9
  77.0 24.9 %all-gather = bf16[1,512,256]{2,1,0:T(8,128)(2,1)S(1)} all-gather(bf16[1,64,256]{2,1,0:T(8,128)(2,1)S(1)} %get-tuple-element.342), channel_id=2, replica_groups=mesh['zonal'=8,'merid'=4] {'zonal'}, dimensions={1}, use_global_device_ids=true | all-gather | bytes 294912 | tf_op jit(solution)/shard_map/all_gather | solution.py:35
  104.7 1.6 scatter-add.101
  107.3 1.6 scatter-add.104
  109.8 1.3 collective-permute-start.10
  111.1 24.5 %all-gather.2 = bf16[1,512,256]{2,1,0:T(8,128)(2,1)S(1)} all-gather(bf16[1,64,256]{2,1,0:T(8,128)(2,1)S(1)} %get-tuple-element.324), channel_id=4, replica_groups=mesh['zonal'=8,'merid'=4] {'zonal'}, dimensions={1}, use_global_device_ids=true | all-gather | bytes 294912 | tf_op jit(solution)/shard_map/all_gather | solution.py:42
  135.6 1.3 slice.1039
  137.0 16.1 %collective-permute-start.11 = (bf16[1,64,256]{2,1,0:T(8,128)(2,1)S(1)}, bf16[1,64,256]{2,1,0:T(8,128)(2,1)S(1)}, u32[]{:S(2)}, u32[]{:S(2)}) collective-permute-start(bf16[1,64,256]{2,1,0:T(8,128)(2,1)S(1)} %get-tuple-element.325), channel_id=1, source_target_pairs={{1,0},{2,1},{3,2},{5,4},{6,5},{7,6},{9,8},{10,9},{11,10},{13,12},{... | collective-permute-start | bytes 98312 | tf_op jit(solution)/shard_map/ppermute | solution.py:21
  154.6 4.2 collective-permute-start.3
  163.3 1.5 copy-done.11
  164.8 3.3 fusion.8
  168.1 1.4 fusion.33
  169.6 3.6 copy-done.2
  173.2 2.3 fusion.18
  175.7 6.8 %copy.30 = bf16[2304,1024]{1,0:T(8,128)(2,1)} copy(bf16[2304,1024]{0,1:T(8,128)(2,1)} %bitcast.164) | data formatting | bytes 9437184 | tf_op jit(solution)/shard_map/dot_general | solution.py:96
  182.4 3.7 collective-permute-start.5
  186.1 1.5 collective-permute-start.4
  187.6 3.2 scatter-add.110
  190.8 3.3 add_select_fusion
  194.0 3.2 scatter-add.111
  197.2 1.4 fusion.17
  198.7 1.4 fusion.15
  200.1 2.0 scatter-add.115
  202.1 1.4 fusion.14
  203.5 2.0 scatter-add.116
  205.5 1.4 fusion.13
  206.9 1.4 fusion.11
  208.4 5.1 %fusion.55 = f32[3,3,256,256]{3,2,1,0:T(8,128)} fusion(bf16[3,3,256,1024]{3,2,1,0:T(8,128)(2,1)} %bitcast.166, bf16[1024,256,1,1]{1,0,3,2:T(8,128)(2,1)S(1)} %bitcast.173), kind=kOutput, calls=%fused_computation.154 | convolution fusion | flops 1207959552 | bytes 7602176 | tf_op jit(solution)/shard_map/dot_general | solution.py:96
  213.5 26.6 %all-gather.1 = bf16[1,512,256]{2,1,0:T(8,128)(2,1)} all-gather(bf16[1,64,256]{2,1,0:T(8,128)(2,1)S(1)} %get-tuple-element.340), channel_id=3, replica_groups=mesh['zonal'=8,'merid'=4] {'zonal'}, dimensions={1}, use_global_device_ids=true | all-gather | bytes 294912 | tf_op jit(solution)/shard_map/all_gather | solution.py:35
  240.2 1.8 gather_fusion.1
  241.9 2.0 scatter-add.120
  244.9 1.5 collective-permute-start.6
  246.4 2.8 collective-permute-start.7
  249.1 1.4 fusion.10
  250.5 2.0 scatter-add.121
  255.5 2.2 copy-done.6
  257.6 6.7 %copy.31 = bf16[2304,1024]{1,0:T(8,128)(2,1)} copy(bf16[2304,1024]{0,1:T(8,128)(2,1)} %bitcast.165) | data formatting | bytes 9437184 | tf_op jit(solution)/shard_map/dot_general | solution.py:96
  264.3 5.1 %fusion.56 = f32[3,3,256,256]{3,2,1,0:T(8,128)} fusion(bf16[3,3,256,1024]{3,2,1,0:T(8,128)(2,1)} %bitcast.167, bf16[1024,256,1,1]{1,0,3,2:T(8,128)(2,1)S(1)} %bitcast.168), kind=kOutput, calls=%fused_computation.155 | convolution fusion | flops 1207959552 | bytes 7602176 | tf_op jit(solution)/shard_map/dot_general | solution.py:96
  270.5 4.1 collective-permute-start.13
  276.3 1.3 collective-permute-start.14
  277.6 11.7 %collective-permute-start.15 = (bf16[1,64,256]{2,1,0:T(8,128)(2,1)S(1)}, bf16[1,64,256]{2,1,0:T(8,128)(2,1)S(1)}, u32[]{:S(2)}, u32[]{:S(2)}) collective-permute-start(bf16[1,64,256]{2,1,0:T(8,128)(2,1)S(1)} %get-tuple-element.323), channel_id=1, source_target_pairs={{1,0},{2,1},{3,2},{5,4},{6,5},{7,6},{9,8},{10,9},{11,10},{13,12},{... | collective-permute-start | bytes 98312 | tf_op jit(solution)/shard_map/ppermute | solution.py:21
  289.3 25.7 %all-gather.3 = bf16[1,512,256]{2,1,0:T(8,128)(2,1)S(1)} all-gather(bf16[1,64,256]{2,1,0:T(8,128)(2,1)S(1)} %get-tuple-element.322), channel_id=5, replica_groups=mesh['zonal'=8,'merid'=4] {'zonal'}, dimensions={1}, use_global_device_ids=true | all-gather | bytes 294912 | tf_op jit(solution)/shard_map/all_gather | solution.py:42
  315.8 5.2 %fusion.1 = bf16[16,64,256]{2,1,0:T(8,128)(2,1)} fusion(bf16[16,64,2304]{2,1,0:T(8,128)(2,1)} %copy-done.6, bf16[2304,256,1]{1,0,2:T(8,128)(2,1)} %bitcast.170, bf16[16,64,256]{2,1,0:T(8,128)(2,1)S(1)} %copy-done.4, f32[256]{0:T(256)S(1)} %copy-done.24, s32[16,64]{1,0:T(8,128)S(1)} %copy-done.15, s32[256]{0:T(256)S(1)} %copy-done.21), kind=kOutput, calls=%fused_computation.15 | convolution fusion | flops 1209532416 | bytes 6952960 | tf_op jit(solution)/shard_map/dot_general | solution.py:119
  322.2 97.6 %all-reduce.5.cloned.1.call-done = (f32[3,3,256,256]{3,2,1,0:T(8,128)}, f32[3,3,256,256]{3,2,1,0:T(8,128)}) async-done(((f32[3,3,256,256]{3,2,1,0:T(8,128)}, f32[3,3,256,256]{3,2,1,0:T(8,128)}), (f32[3,3,256,256]{3,2,1,0:T(8,128)}, f32[3,3,256,256]{3,2,1,0:T(8,128)})) %all-reduce.5.cloned.1.call-update) | async-done | bytes 4718608 | tf_op jit(solution)/shard_map/psum | solution.py:138
  419.9 5.2 %broadcast_multiply_fusion = (f32[3,3,256,256]{3,2,1,0:T(8,128)}, f32[3,3,256,256]{3,2,1,0:T(8,128)}) fusion(f32[3,3,256,256]{3,2,1,0:T(8,128)} %get-tuple-element.319, f32[3,3,256,256]{3,2,1,0:T(8,128)} %get-tuple-element.318), kind=kLoop, calls=%fused_computation.16 | loop fusion | flops 1179648 | bytes 9437184 | tf_op jit(solution)/shard_map/mul | solution.py:140
  (130 shorter events, 23.4 us)
Async XLA Ops:
  7.2 157.6 %copy-start = (bf16[3,3,256,256]{3,2,1,0:T(8,128)(2,1)S(1)}, bf16[3,3,256,256]{3,2,1,0:T(8,128)(2,1)}, u32[]{:S(2)}) copy-start(bf16[3,3,256,256]{3,2,1,0:T(8,128)(2,1)} %param.65) | copy-start | bytes 3538948
  7.2 412.7 %all-reduce.5.cloned.1.call-start = ((), (), s32[]{:S(2)}) async-start(), calls=%async_computation | async-start | bytes 9437184 | tf_op jit(solution)/shard_map/psum | solution.py:138
  8.7 144.4 %collective-permute-start.1 = (bf16[1,64,256]{2,1,0:T(8,128)(2,1)}, bf16[1,64,256]{2,1,0:T(8,128)(2,1)}, u32[]{:S(2)}, u32[]{:S(2)}) collective-permute-start(bf16[1,64,256]{2,1,0:T(8,128)(2,1)} %get-tuple-element.343), channel_id=1, source_target_pairs={{1,0},{2,1},{3,2},{5,4},{6,5},{7,6},{9,8},{10,9},{11,10},{13,12},{... | collective-permute-start | bytes 98312 | tf_op jit(solution)/shard_map/ppermute | solution.py:21
  11.9 142.1 %collective-permute-start = (bf16[1,64,256]{2,1,0:T(8,128)(2,1)S(1)}, bf16[1,64,256]{2,1,0:T(8,128)(2,1)S(1)}, u32[]{:S(2)}, u32[]{:S(2)}) collective-permute-start(bf16[1,64,256]{2,1,0:T(8,128)(2,1)S(1)} %get-tuple-element.342), channel_id=1, source_target_pairs={{0,1},{1,2},{2,3},{4,5},{5,6},{6,7},{8,9},{9,10},{10,11},{12,13},{... | collective-permute-start | bytes 98312 | tf_op jit(solution)/shard_map/ppermute | solution.py:19
  13.2 4.2 copy-start.19
  14.5 2.9 copy-start.8
  17.4 4.5 %copy-start.3 = (f32[16,64,9,256]{3,1,0,2:T(8,128)}, f32[16,64,9,256]{3,1,0,2:T(8,128)S(1)}, u32[]{:S(2)}) copy-start(f32[16,64,9,256]{3,1,0,2:T(8,128)S(1)} %fusion.35) | copy-start | bytes 28311556
  19.4 2.5 copy-start.22
  72.6 31.9 %collective-permute-start.8 = (bf16[18,1,256]{2,1,0:T(2,128)(2,1)S(1)}, bf16[18,1,256]{2,1,0:T(2,128)(2,1)S(1)}, u32[]{:S(2)}, u32[]{:S(2)}) collective-permute-start(bf16[18,1,256]{2,1,0:T(2,128)(2,1)S(1)} %get-tuple-element.330), channel_id=1, source_target_pairs={{0,4},{4,8},{8,12},{12,16},{16,20},{20,24},{24,28},{28,0},{1,5},{5... | collective-permute-start | bytes 27656 | tf_op jit(solution)/shard_map/ppermute | solution.py:19
  73.9 30.7 %collective-permute-start.9 = (bf16[18,1,256]{2,1,0:T(2,128)(2,1)S(1)}, bf16[18,1,256]{2,1,0:T(2,128)(2,1)S(1)}, u32[]{:S(2)}, u32[]{:S(2)}) collective-permute-start(bf16[18,1,256]{2,1,0:T(2,128)(2,1)S(1)} %get-tuple-element.331), channel_id=1, source_target_pairs={{4,0},{8,4},{12,8},{16,12},{20,16},{24,20},{28,24},{0,28},{5,1},{9... | collective-permute-start | bytes 27656 | tf_op jit(solution)/shard_map/ppermute | solution.py:21
  102.6 60.6 %copy-start.16 = (pred[64]{0:T(512)(128)(4,1)}, pred[64]{0:T(512)(128)(4,1)S(1)}, u32[]{:S(2)}) copy-start(pred[64]{0:T(512)(128)(4,1)S(1)} %get-tuple-element.320) | copy-start | bytes 196
  102.7 56.2 %copy-start.18 = (s32[1024]{0:T(1024)}, s32[1024]{0:T(1024)S(1)}, u32[]{:S(2)}) copy-start(s32[1024]{0:T(1024)S(1)} %pad_clamp_fusion) | copy-start | bytes 12292
  102.7 51.3 %copy-start.4 = (bf16[16,64,256]{2,1,0:T(8,128)(2,1)S(1)}, bf16[16,64,256]{2,1,0:T(8,128)(2,1)}, u32[]{:S(2)}) copy-start(bf16[16,64,256]{2,1,0:T(8,128)(2,1)} %param.64) | copy-start | bytes 1572868
  109.8 52.4 %collective-permute-start.10 = (bf16[1,64,256]{2,1,0:T(8,128)(2,1)S(1)}, bf16[1,64,256]{2,1,0:T(8,128)(2,1)S(1)}, u32[]{:S(2)}, u32[]{:S(2)}) collective-permute-start(bf16[1,64,256]{2,1,0:T(8,128)(2,1)S(1)} %get-tuple-element.324), channel_id=1, source_target_pairs={{0,1},{1,2},{2,3},{4,5},{5,6},{6,7},{8,9},{9,10},{10,11},{12,13},{... | collective-permute-start | bytes 98312 | tf_op jit(solution)/shard_map/ppermute | solution.py:19
  137.0 25.3 %collective-permute-start.11 = (bf16[1,64,256]{2,1,0:T(8,128)(2,1)S(1)}, bf16[1,64,256]{2,1,0:T(8,128)(2,1)S(1)}, u32[]{:S(2)}, u32[]{:S(2)}) collective-permute-start(bf16[1,64,256]{2,1,0:T(8,128)(2,1)S(1)} %get-tuple-element.325), channel_id=1, source_target_pairs={{1,0},{2,1},{3,2},{5,4},{6,5},{7,6},{9,8},{10,9},{11,10},{13,12},{... | collective-permute-start | bytes 98312 | tf_op jit(solution)/shard_map/ppermute | solution.py:21
  154.6 5.6 %collective-permute-start.2 = (bf16[18,1,256]{2,1,0:T(2,128)(2,1)}, bf16[18,1,256]{2,1,0:T(2,128)(2,1)}, u32[]{:S(2)}, u32[]{:S(2)}) collective-permute-start(bf16[18,1,256]{2,1,0:T(2,128)(2,1)} %get-tuple-element.339), channel_id=1, source_target_pairs={{0,4},{4,8},{8,12},{12,16},{16,20},{20,24},{24,28},{28,0},{1,5},{5... | collective-permute-start | bytes 27656 | tf_op jit(solution)/shard_map/ppermute | solution.py:19
  154.6 5.6 %collective-permute-start.3 = (bf16[18,1,256]{2,1,0:T(2,128)(2,1)}, bf16[18,1,256]{2,1,0:T(2,128)(2,1)}, u32[]{:S(2)}, u32[]{:S(2)}) collective-permute-start(bf16[18,1,256]{2,1,0:T(2,128)(2,1)} %get-tuple-element.338), channel_id=1, source_target_pairs={{4,0},{8,4},{12,8},{16,12},{20,16},{24,20},{28,24},{0,28},{5,1},{9... | collective-permute-start | bytes 27656 | tf_op jit(solution)/shard_map/ppermute | solution.py:21
  161.8 3.0 copy-start.14
  161.8 3.0 copy-start.20
  161.8 3.0 copy-start.23
  162.3 5.8 %copy-start.5 = (bf16[16,64,2304]{2,1,0:T(8,128)(2,1)}, bf16[16,64,2304]{2,1,0:T(8,128)(2,1)S(1)}, u32[]{:S(2)}) copy-start(bf16[16,64,2304]{2,1,0:T(8,128)(2,1)S(1)} %slice_dynamic-update-slice_fusion.6) | copy-start | bytes 14155780
  163.3 1.5 copy-start.11
  168.1 1.4 copy-start.12
  169.6 3.7 copy-start.2
  175.6 11.9 %copy-start.7 = (f32[16,64,256]{2,1,0:T(8,128)S(1)}, f32[16,64,256]{2,1,0:T(8,128)}, u32[]{:S(2)}) copy-start(f32[16,64,256]{2,1,0:T(8,128)} %fusion.18) | copy-start | bytes 3145732
  182.4 61.5 %collective-permute-start.5 = (bf16[1,64,256]{2,1,0:T(8,128)(2,1)S(1)}, bf16[1,64,256]{2,1,0:T(8,128)(2,1)}, u32[]{:S(2)}, u32[]{:S(2)}) collective-permute-start(bf16[1,64,256]{2,1,0:T(8,128)(2,1)S(1)} %get-tuple-element.341), channel_id=1, source_target_pairs={{1,0},{2,1},{3,2},{5,4},{6,5},{7,6},{9,8},{10,9},{11,10},{13,12},{... | collective-permute-start | bytes 98312 | tf_op jit(solution)/shard_map/ppermute | solution.py:21
  186.1 58.7 %collective-permute-start.4 = (bf16[1,64,256]{2,1,0:T(8,128)(2,1)S(1)}, bf16[1,64,256]{2,1,0:T(8,128)(2,1)S(1)}, u32[]{:S(2)}, u32[]{:S(2)}) collective-permute-start(bf16[1,64,256]{2,1,0:T(8,128)(2,1)S(1)} %get-tuple-element.340), channel_id=1, source_target_pairs={{0,1},{1,2},{2,3},{4,5},{5,6},{6,7},{8,9},{9,10},{10,11},{12,13},{... | collective-permute-start | bytes 98312 | tf_op jit(solution)/shard_map/ppermute | solution.py:19
  206.9 1.5 copy-start.13
  244.9 8.6 %collective-permute-start.6 = (bf16[18,1,256]{2,1,0:T(2,128)(2,1)S(1)}, bf16[18,1,256]{2,1,0:T(2,128)(2,1)S(1)}, u32[]{:S(2)}, u32[]{:S(2)}) collective-permute-start(bf16[18,1,256]{2,1,0:T(2,128)(2,1)S(1)} %get-tuple-element.335), channel_id=1, source_target_pairs={{0,4},{4,8},{8,12},{12,16},{16,20},{20,24},{24,28},{28,0},{1,5},{5... | collective-permute-start | bytes 27656 | tf_op jit(solution)/shard_map/ppermute | solution.py:19
  246.4 7.1 %collective-permute-start.7 = (bf16[18,1,256]{2,1,0:T(2,128)(2,1)S(1)}, bf16[18,1,256]{2,1,0:T(2,128)(2,1)}, u32[]{:S(2)}, u32[]{:S(2)}) collective-permute-start(bf16[18,1,256]{2,1,0:T(2,128)(2,1)S(1)} %get-tuple-element.334), channel_id=1, source_target_pairs={{4,0},{8,4},{12,8},{16,12},{20,16},{24,20},{28,24},{0,28},{5,1},{9... | collective-permute-start | bytes 27656 | tf_op jit(solution)/shard_map/ppermute | solution.py:21
  255.5 2.2 copy-start.6
  257.6 6.7 %copy-start.9 = (bf16[16,64,256]{2,1,0:T(8,128)(2,1)S(1)}, bf16[16,64,256]{2,1,0:T(8,128)(2,1)}, u32[]{:S(2)}) copy-start(bf16[16,64,256]{2,1,0:T(8,128)(2,1)} %copy-done.8) | copy-start | bytes 1572868
  270.4 5.4 %collective-permute-start.12 = (bf16[18,1,256]{2,1,0:T(2,128)(2,1)S(1)}, bf16[18,1,256]{2,1,0:T(2,128)(2,1)S(1)}, u32[]{:S(2)}, u32[]{:S(2)}) collective-permute-start(bf16[18,1,256]{2,1,0:T(2,128)(2,1)S(1)} %get-tuple-element.328), channel_id=1, source_target_pairs={{0,4},{4,8},{8,12},{12,16},{16,20},{20,24},{24,28},{28,0},{1,5},{5... | collective-permute-start | bytes 27656 | tf_op jit(solution)/shard_map/ppermute | solution.py:19
  270.5 5.3 %collective-permute-start.13 = (bf16[18,1,256]{2,1,0:T(2,128)(2,1)S(1)}, bf16[18,1,256]{2,1,0:T(2,128)(2,1)S(1)}, u32[]{:S(2)}, u32[]{:S(2)}) collective-permute-start(bf16[18,1,256]{2,1,0:T(2,128)(2,1)S(1)} %get-tuple-element.329), channel_id=1, source_target_pairs={{4,0},{8,4},{12,8},{16,12},{20,16},{24,20},{28,24},{0,28},{5,1},{9... | collective-permute-start | bytes 27656 | tf_op jit(solution)/shard_map/ppermute | solution.py:21
  274.8 41.0 %copy-start.15 = (s32[16,64]{1,0:T(8,128)S(1)}, s32[16,64]{1,0:T(8,128)}, u32[]{:S(2)}) copy-start(s32[16,64]{1,0:T(8,128)} %param.69) | copy-start | bytes 12292
  274.8 41.0 %copy-start.21 = (s32[256]{0:T(256)S(1)}, s32[256]{0:T(256)}, u32[]{:S(2)}) copy-start(s32[256]{0:T(256)} %copy-done.19) | copy-start | bytes 3076
  274.8 41.0 %copy-start.24 = (f32[256]{0:T(256)S(1)}, f32[256]{0:T(256)}, u32[]{:S(2)}) copy-start(f32[256]{0:T(256)} %param.68) | copy-start | bytes 3076
  276.3 44.7 %collective-permute-start.14 = (bf16[1,64,256]{2,1,0:T(8,128)(2,1)S(1)}, bf16[1,64,256]{2,1,0:T(8,128)(2,1)S(1)}, u32[]{:S(2)}, u32[]{:S(2)}) collective-permute-start(bf16[1,64,256]{2,1,0:T(8,128)(2,1)S(1)} %get-tuple-element.322), channel_id=1, source_target_pairs={{0,1},{1,2},{2,3},{4,5},{5,6},{6,7},{8,9},{9,10},{10,11},{12,13},{... | collective-permute-start | bytes 98312 | tf_op jit(solution)/shard_map/ppermute | solution.py:19
  277.6 43.4 %collective-permute-start.15 = (bf16[1,64,256]{2,1,0:T(8,128)(2,1)S(1)}, bf16[1,64,256]{2,1,0:T(8,128)(2,1)S(1)}, u32[]{:S(2)}, u32[]{:S(2)}) collective-permute-start(bf16[1,64,256]{2,1,0:T(8,128)(2,1)S(1)} %get-tuple-element.323), channel_id=1, source_target_pairs={{1,0},{2,1},{3,2},{5,4},{6,5},{7,6},{9,8},{10,9},{11,10},{13,12},{... | collective-permute-start | bytes 98312 | tf_op jit(solution)/shard_map/ppermute | solution.py:21
  315.8 5.2 %copy-start.17 = (pred[64]{0:T(512)(128)(4,1)S(1)}, pred[64]{0:T(512)(128)(4,1)}, u32[]{:S(2)}) copy-start(pred[64]{0:T(512)(128)(4,1)} %copy-done.16) | copy-start | bytes 196
  315.8 5.3 %copy-start.10 = (bf16[16,64,256]{2,1,0:T(8,128)(2,1)S(1)}, bf16[16,64,256]{2,1,0:T(8,128)(2,1)}, u32[]{:S(2)}) copy-start(bf16[16,64,256]{2,1,0:T(8,128)(2,1)} %param.71) | copy-start | bytes 1572868
  419.9 5.2 %copy-start.1 = (bf16[3,3,256,256]{3,2,1,0:T(8,128)(2,1)S(1)}, bf16[3,3,256,256]{3,2,1,0:T(8,128)(2,1)}, u32[]{:S(2)}) copy-start(bf16[3,3,256,256]{3,2,1,0:T(8,128)(2,1)} %param.65) | copy-start | bytes 3538948
Sparse Core Ops, SparseCore 0:
  269.6 150.2 all-reduce.4
where the time goes:
time: 437 us; the launch traced here: 432 us
  blocking collectives  102 us (23%)
  waiting for transfers between devices  99.4 us (23%)
  local copies, waits for them, and re-layouts  85.4 us (20%)
  starting transfers between devices  57 us (13%)
  other arithmetic  50.4 us (12%)
  matrix products  23.1 us (5%)
  between operations  15 us (3%)
    psum x1, waiting for transfers between devices, shards(): grad_one, grad_two = lax.psum((grad_one, grad_two), ('zonal', 'merid'))  97.6 us
    all_gather x2, blocking collectives, fold_forward(): whole_row = lax.all_gather(top_row, 'zonal', axis=0, tiled=True)  51.6 us
    all_gather x2, blocking collectives, fold_backward(): lax.all_gather(fold_grad.astype(jnp.bfloat16), 'zonal', axis=0, tiled=True)  50.2 us
    ppermute x8, starting transfers between devices, with_halo(): lax.ppermute(head, axis, [((i + 1) % count, i) for i in range(ends)])  48.8 us
    scatter-add x14, local copies, waits for them, and re-layouts, transpose_conv(): grad_pad.at[row_step:row_step + rows, col_step:col_step + columns]  47.8 us
    add x10, other arithmetic, transpose_conv(): grad_pad.at[row_step:row_step + rows, col_step:col_step + columns]  19.7 us
    dot_general x2, local copies, waits for them, and re-layouts, kernel_grad(): lax.dot_general(patches, delta, (((0,), (0,)), ((), ())), preferred_eleme...  13.4 us
    dot_general x2, matrix products, kernel_grad(): lax.dot_general(patches, delta, (((0,), (0,)), ((), ())), preferred_eleme...  10.3 us
  transfers between devices with their start and end apart: 17, of which 3 were waited for; matrix products, arithmetic and copies ran while one was open for 27% of the time, Pallas kernels for 0%

commit v1 on v0

v1 whole, which is shorter than its diff:
```python
import functools
import math

import jax
import jax.numpy as jnp
from jax import lax
from jax.experimental import pallas as pl
from jax.experimental.pallas import tpu as pltpu
from jax.sharding import PartitionSpec as P

LEV = 64
MESH = pl.DeviceIdType.MESH
BF = jnp.bfloat16
F32 = jnp.float32
GELU_A = math.sqrt(2.0 / math.pi)
GELU_B = 0.044715


def plan_steps(total, nz, nm):
    merid_bits = [("merid", 1 << i) for i in range(nm.bit_length() - 1)]
    zonal_bits = [("zonal", 1 << i) for i in range(nz.bit_length() - 1)]
    order_one = merid_bits + zonal_bits
    order_two = merid_bits[:1] + zonal_bits[1:2] + merid_bits[1:] + zonal_bits[:1] + zonal_bits[2:]
    plans = []
    for order in (order_one, order_two):
        size, plan = total, []
        for step, (axis, bit) in enumerate(order):
            halve = size % 32 == 0
            if halve:
                size //= 2
            plan.append((axis, bit, size, halve, step == 0 or step > 2))
        plans.append(plan)
    return plans


def kernel(
    nz, nm, rows, cols, plans,
    field, delta_in, mask, w_one, b_one, w_two, b_two, partner_tab,
    out, in_grad, sums,
    va, vb, gp, hg,
    q_field, q_hidden, q_two, q_one, ql_two, ql_one, wt_one, wt_two, wl_one, wl_two,
    west, east, north, south, cols32,
    row_send, col_send, row_recv, col_recv, fold_all, acc, ar_send, ar_recv, ar_wide,
    halo_ss, halo_rs, fold_ss, fold_rs, ar_ss, ar_rs, ag_ss, ag_rs,
):
    ch = field.shape[1]
    cells = rows * cols
    z = lax.axis_index("zonal")
    m = lax.axis_index("merid")
    zw = (z + nz - 1) % nz
    ze = (z + 1) % nz
    has_n = m < nm - 1
    has_s = m > 0
    is_top = m == nm - 1

    def partner_of(axis, bit):
        index = z if axis == "zonal" else m
        mine = (index // bit) % 2
        other = index + bit - 2 * bit * mine
        if axis == "zonal":
            return mine, {"zonal": other, "merid": m}
        return mine, {"zonal": z, "merid": other}

    barrier = pltpu.get_barrier_semaphore()

    def greet(mm, zz):
        pl.semaphore_signal(
            barrier, 1, device_id={"zonal": zz, "merid": mm}, device_id_type=MESH
        )

    greet(m, zw)
    greet(m, ze)
    for axis, bit, _, _, _ in plans[0]:
        _, other = partner_of(axis, bit)
        greet(other["merid"], other["zonal"])

    @pl.when(has_n)
    def _():
        for zz in (zw, z, ze):
            greet(m + 1, zz)

    @pl.when(has_s)
    def _():
        for zz in (zw, z, ze):
            greet(m - 1, zz)

    @pl.when(is_top)
    def _():
        @pl.loop(1, nz)
        def _(k):
            greet(m, (z + k) % nz)

    def copy_to(src, dst, ssem, rsem, mm, zz):
        return pltpu.make_async_remote_copy(
            src_ref=src, dst_ref=dst, send_sem=ssem, recv_sem=rsem,
            device_id={"zonal": zz, "merid": mm}, device_id_type=MESH,
        )

    def col_copy(p, slot, mm, zz):
        src = col_send.at[p, 0 if slot < 3 else 1]
        return copy_to(src, col_recv.at[p, slot], halo_ss.at[p, slot], halo_rs.at[p, slot], mm, zz)

    def row_copy(p, slot, mm, zz):
        return copy_to(
            row_send.at[p, slot], row_recv.at[p, slot],
            halo_ss.at[p, 6 + slot], halo_rs.at[p, 6 + slot], mm, zz,
        )

    def fold_copy(p, source, target):
        return copy_to(
            row_send.at[p, 0], fold_all.at[p, source],
            fold_ss.at[p, target], fold_rs.at[p, source], m, target,
        )

    def prepare(p):
        for k, v in enumerate((va, vb)):
            row_send[p, 0, k * cols:(k + 1) * cols, :] = v[cells - cols:, :].astype(BF)
            row_send[p, 1, k * cols:(k + 1) * cols, :] = v[:cols, :].astype(BF)
            for side, x in ((0, cols - 1), (1, 0)):
                for y in range(rows):
                    cols32[y:y + 1, :] = v[y * cols + x:y * cols + x + 1, :]
                col_send[p, side, k * rows:(k + 1) * rows, :] = cols32[...].astype(BF)

    def halo(p, what):
        def act(copy):
            getattr(copy, what)()

        act(col_copy(p, 0, m, ze))
        act(col_copy(p, 3, m, zw))

        @pl.when(has_n)
        def _():
            act(row_copy(p, 0, m + 1, z))
            act(col_copy(p, 1, m + 1, ze))
            act(col_copy(p, 4, m + 1, zw))

        @pl.when(has_s)
        def _():
            act(row_copy(p, 1, m - 1, z))
            act(col_copy(p, 2, m - 1, ze))
            act(col_copy(p, 5, m - 1, zw))

        @pl.when(is_top)
        def _():
            @pl.loop(1, nz)
            def _(k):
                act(fold_copy(p, z, (z + k) % nz))

    def halo_arrive(p):
        col_copy(p, 0, m, ze).wait_recv()
        col_copy(p, 3, m, zw).wait_recv()

        @pl.when(has_s)
        def _():
            row_copy(p, 0, m, ze).wait_recv()
            col_copy(p, 1, m, ze).wait_recv()
            col_copy(p, 4, m, zw).wait_recv()

        @pl.when(has_n)
        def _():
            row_copy(p, 1, m, ze).wait_recv()
            col_copy(p, 2, m, ze).wait_recv()
            col_copy(p, 5, m, zw).wait_recv()

        @pl.when(is_top)
        def _():
            fold_all[p, z, :, :] = row_send[p, 0, :, :]

            @pl.loop(1, nz)
            def _(k):
                fold_copy(p, (z + nz - k) % nz, ze).wait_recv()

    spot = lax.broadcasted_iota(jnp.int32, (cols, ch), 0)

    def emit(row, wrow, erow, q, off):
        left = jnp.where(spot == 0, wrow, pltpu.roll(row, 1, 0))
        right = jnp.where(spot == cols - 1, erow, pltpu.roll(row, cols - 1, 0))
        q[pl.ds(off, cols), 0:ch] = left.astype(BF)
        q[pl.ds(off, cols), ch:2 * ch] = row.astype(BF)
        q[pl.ds(off, cols), 2 * ch:3 * ch] = right.astype(BF)

    def assemble(p, k, v, q, ql):
        mine = slice(k * rows, (k + 1) * rows)
        span = slice(k * cols, (k + 1) * cols)
        west[0:rows, :] = col_recv[p, 0, mine, :].astype(F32)
        east[0:rows, :] = col_recv[p, 3, mine, :].astype(F32)

        @pl.when(has_s)
        def _():
            south[...] = row_recv[p, 0, span, :].astype(F32)
            west[rows:rows + 1, :] = col_recv[p, 1, mine, :].astype(F32)[rows - 1:rows, :]
            east[rows:rows + 1, :] = col_recv[p, 4, mine, :].astype(F32)[rows - 1:rows, :]

        @pl.when(jnp.logical_not(has_s))
        def _():
            south[...] = jnp.zeros_like(south)
            west[rows:rows + 1, :] = jnp.zeros((1, ch), F32)
            east[rows:rows + 1, :] = jnp.zeros((1, ch), F32)

        @pl.when(has_n)
        def _():
            north[...] = row_recv[p, 1, span, :].astype(F32)
            west[rows + 1:rows + 2, :] = col_recv[p, 2, mine, :].astype(F32)[0:1, :]
            east[rows + 1:rows + 2, :] = col_recv[p, 5, mine, :].astype(F32)[0:1, :]

        @pl.when(is_top)
        def _():
            around = nz * cols
            extra = cols + 16
            first = partner_tab[0]
            at = lax.broadcasted_iota(jnp.int32, (extra, around), 0)
            column = z * cols + jnp.where(at < cols, at, jnp.where(at == cols, -1, cols))
            target = first - column
            target = jnp.where(target < 0, target + around, target)
            target = jnp.where(target >= around, target - around, target)
            source = lax.broadcasted_iota(jnp.int32, (extra, around), 1)
            pick = jnp.where(target == source, 1.0, 0.0).astype(BF)
            whole_row = fold_all[p, :, span, :].reshape(around, ch)
            folded = jnp.dot(pick, whole_row, preferred_element_type=F32)
            north[...] = folded[0:cols, :]
            west[rows + 1:rows + 2, :] = folded[cols:cols + 1, :]
            east[rows + 1:rows + 2, :] = folded[cols + 1:cols + 2, :]

        @pl.loop(0, rows)
        def _(y):
            off = pl.multiple_of(y * cols, cols)
            emit(
                v[pl.ds(off, cols), :], west[pl.ds(y, 1), :], east[pl.ds(y, 1), :],
                q, pl.multiple_of(off + cols, cols),
            )

        emit(south[...], west[rows:rows + 1, :], east[rows:rows + 1, :], q, 0)
        if ql is None:
            emit(north[...], west[rows + 1:rows + 2, :], east[rows + 1:rows + 2, :], q, cells + cols)
        else:
            emit(north[...], west[rows + 1:rows + 2, :], east[rows + 1:rows + 2, :], ql, 0)
            q[cells + cols:, :] = jnp.zeros((cols, 3 * ch), BF)

    chunk = 4 * cols

    def conv(q, w, finish):
        @pl.loop(0, cells // chunk)
        def _(i):
            off = pl.multiple_of(i * chunk, chunk)
            total = jnp.dot(q[pl.ds(off, chunk), :], w[0], preferred_element_type=F32)
            for a in (1, 2):
                at = pl.multiple_of(off + a * cols, cols)
                total += jnp.dot(q[pl.ds(at, chunk), :], w[a], preferred_element_type=F32)
            finish(pl.ds(off, chunk), total)

    def transpose_weights(w, wt, wl):
        @pl.loop(0, 3)
        def _(a):
            for b in range(3):
                turned = w[2 - a, (2 - b) * ch:(3 - b) * ch, :].astype(F32).T
                wt[a, b * ch:(b + 1) * ch, :] = turned.astype(BF)

        for b in range(3):
            @pl.when(is_top)
            def _():
                wl[b * ch:(b + 1) * ch, :] = wt[0, (2 - b) * ch:(3 - b) * ch, :]

            @pl.when(jnp.logical_not(is_top))
            def _():
                wl[b * ch:(b + 1) * ch, :] = wt[2, b * ch:(b + 1) * ch, :]

    def last_row(ql, wl, target):
        target[cells - cols:, :] += jnp.dot(ql[...], wl[...], preferred_element_type=F32)

    def gradient(g, q, e_turned):
        for a in range(3):
            for b in range(3):
                part = jnp.dot(
                    e_turned, q[a * cols:a * cols + cells, b * ch:(b + 1) * ch],
                    preferred_element_type=F32,
                )
                acc[g, (3 * a + b) * ch:(3 * a + b + 1) * ch, :] = part.T

    def loop_rows(count, body):
        piece = 48 if count % 48 == 0 else 16

        @pl.loop(0, count // piece)
        def _(i):
            body(i * piece, piece)

    def reduce_all(g):
        low = 0
        place = 0
        place_wide = 0
        waits = []
        gathers = []
        for step, (axis, bit, size, halve, wide) in enumerate(plans[g]):
            mine, other = partner_of(axis, bit)
            keep = low + mine * size if halve else low
            give = low + (1 - mine) * size if halve else low
            if halve:
                gathers.append((step, axis, bit, size, low))

            def fill(off, piece, give=give, place=place):
                ar_send[g, pl.ds(place + pl.multiple_of(off, 16), piece), :] = acc[
                    g, pl.ds(pl.multiple_of(give + off, 16), piece), :
                ].astype(BF)

            if wide:
                source = acc.at[g, pl.ds(pl.multiple_of(give, 16), size)]
                landing, start = ar_wide, place_wide
                place_wide += size
            else:
                loop_rows(size, fill)
                source = ar_send.at[g, pl.ds(place, size)]
                landing, start = ar_recv, place
            copy = copy_to(
                source, landing.at[g, pl.ds(start, size)],
                ar_ss.at[g, step], ar_rs.at[g, step], other["merid"], other["zonal"],
            )
            copy.start()
            yield
            copy.wait_recv()
            if wide and not halve:
                copy.wait_send()
            else:
                waits.append(copy)

            def add(
                off, piece, keep=keep, place=place, rounded=not (halve or wide),
                landing=landing, start=start,
            ):
                at = pl.ds(pl.multiple_of(keep + off, 16), piece)
                here = pl.ds(start + pl.multiple_of(off, 16), piece)
                own = ar_send[g, here, :].astype(F32) if rounded else acc[g, at, :]
                acc[g, at, :] = own + landing[g, here, :].astype(F32)

            loop_rows(size, add)
            if not wide:
                place += size
            low = keep
        final = plans[g][-1][2]

        def settle(off, piece, low=low):
            at = pl.ds(pl.multiple_of(low + off, 16), piece)
            sums[g, at, :] = acc[g, at, :].astype(BF)

        loop_rows(final, settle)
        size = final
        for step, axis, bit, size, base in reversed(gathers):
            mine, other = partner_of(axis, bit)
            at = pl.ds(pl.multiple_of(base + mine * size, 16), size)
            theirs = pl.ds(pl.multiple_of(base + (1 - mine) * size, 16), size)
            copy = copy_to(
                sums.at[g, at], sums.at[g, at], ag_ss.at[g, step], ag_rs.at[g, step],
                other["merid"], other["zonal"],
            )
            copy.start()
            waits.append(copy)
            yield
            copy_to(
                sums.at[g, theirs], sums.at[g, theirs], ag_ss.at[g, step], ag_rs.at[g, step],
                other["merid"], other["zonal"],
            ).wait_recv()
        for copy in waits:
            copy.wait_send()

    va[...] = field[...].astype(F32)
    vb[...] = delta_in[...].astype(F32)
    prepare(0)
    count = (
        2 + len(plans[0]) + jnp.where(has_n, 3, 0) + jnp.where(has_s, 3, 0)
        + jnp.where(is_top, nz - 1, 0)
    )
    pl.semaphore_wait(barrier, count)
    halo(0, "start")
    transpose_weights(w_two, wt_two, wl_two)
    transpose_weights(w_one, wt_one, wl_one)
    halo_arrive(0)
    assemble(0, 0, va, q_field, None)
    assemble(0, 1, vb, q_two, ql_two)

    def finish_one(at, total):
        x = total + b_one[...]
        keep = mask[at, :].astype(F32)
        square = x * x
        t = jnp.tanh(GELU_A * x * (1.0 + GELU_B * square))
        half = 0.5 * (1.0 + t)
        va[at, :] = (x * half * keep).astype(BF).astype(F32)
        slope = half + 0.5 * x * (1.0 - t * t) * (GELU_A * (1.0 + 3.0 * GELU_B * square))
        gp[at, :] = slope * keep

    conv(q_field, w_one, finish_one)

    def finish_hg(at, total):
        hg[at, :] = total

    conv(q_two, wt_two, finish_hg)
    last_row(ql_two, wl_two, hg)

    @pl.loop(0, rows)
    def _(y):
        at = pl.ds(pl.multiple_of(y * cols, cols), cols)
        vb[at, :] = (gp[at, :] * hg[at, :]).astype(BF).astype(F32)

    prepare(1)
    halo(1, "start")

    gradient(0, q_field, vb[...].T.astype(BF))
    first = reduce_all(0)
    next(first)
    halo_arrive(1)
    assemble(1, 0, va, q_hidden, None)
    assemble(1, 1, vb, q_one, ql_one)
    next(first)
    gradient(1, q_hidden, delta_in[...].astype(F32).T.astype(BF))
    second = reduce_all(1)
    next(second)

    def advance(gen):
        return next(gen, "end") != "end"

    advance(first)
    advance(second)

    def finish_out(at, total):
        full = field[at, :].astype(F32) + total + b_two[...]
        out[at, :] = (full * mask[at, :].astype(F32)).astype(BF)

    conv(q_hidden, w_two, finish_out)
    advance(first)
    advance(second)
    conv(q_one, wt_one, finish_hg)
    last_row(ql_one, wl_one, hg)

    @pl.loop(0, rows)
    def _(y):
        at = pl.ds(pl.multiple_of(y * cols, cols), cols)
        in_grad[at, :] = (delta_in[at, :].astype(F32) + hg[at, :]).astype(BF)

    more = True
    while more:
        one = advance(first)
        two = advance(second)
        more = one or two
    halo(0, "wait_send")
    halo(1, "wait_send")


def shards(
    field, weight_one, bias_one, weight_two, bias_two, depth_levels, fold_partner, cotangent,
    nz, nm,
):
    rows, cols, ch = field.shape
    cells = rows * cols
    total = 9 * ch
    level = lax.broadcasted_iota(jnp.int32, (1, 1, ch), 2) % LEV
    mask = (level < depth_levels[:, :, None]).astype(BF)
    delta = cotangent * mask
    plans = plan_steps(total, nz, nm)
    sent = max(sum(step[2] for step in plan if not step[4]) for plan in plans)
    sent_wide = max(sum(step[2] for step in plan if step[4]) for plan in plans)
    steps = len(plans[0])
    vmem = pl.BlockSpec(memory_space=pltpu.VMEM)
    smem = pl.BlockSpec(memory_space=pltpu.SMEM)
    wide = 3 * ch
    dma = pltpu.SemaphoreType.DMA
    out, in_grad, sums = pl.pallas_call(
        functools.partial(kernel, nz, nm, rows, cols, plans),
        out_shape=(
            jax.ShapeDtypeStruct((cells, ch), BF),
            jax.ShapeDtypeStruct((cells, ch), BF),
            jax.ShapeDtypeStruct((2, total, ch), BF),
        ),
        in_specs=[vmem] * 7 + [smem],
        out_specs=(vmem, vmem, vmem),
        scratch_shapes=[
            pltpu.VMEM((cells, ch), F32), pltpu.VMEM((cells, ch), F32),
            pltpu.VMEM((cells, ch), F32), pltpu.VMEM((cells, ch), F32),
            pltpu.VMEM((cells + 2 * cols, wide), BF), pltpu.VMEM((cells + 2 * cols, wide), BF),
            pltpu.VMEM((cells + 2 * cols, wide), BF), pltpu.VMEM((cells + 2 * cols, wide), BF),
            pltpu.VMEM((cols, wide), BF), pltpu.VMEM((cols, wide), BF),
            pltpu.VMEM((3, wide, ch), BF), pltpu.VMEM((3, wide, ch), BF),
            pltpu.VMEM((wide, ch), BF), pltpu.VMEM((wide, ch), BF),
            pltpu.VMEM((rows + 8, ch), F32), pltpu.VMEM((rows + 8, ch), F32),
            pltpu.VMEM((cols, ch), F32), pltpu.VMEM((cols, ch), F32),
            pltpu.VMEM((rows, ch), F32),
            pltpu.VMEM((2, 2, 2 * cols, ch), BF), pltpu.VMEM((2, 2, 2 * rows, ch), BF),
            pltpu.VMEM((2, 2, 2 * cols, ch), BF), pltpu.VMEM((2, 6, 2 * rows, ch), BF),
            pltpu.VMEM((2, nz, 2 * cols, ch), BF),
            pltpu.VMEM((2, total, ch), F32),
            pltpu.VMEM((2, sent, ch), BF), pltpu.VMEM((2, sent, ch), BF),
            pltpu.VMEM((2, sent_wide, ch), F32),
            dma((2, 8)), dma((2, 8)), dma((2, nz)), dma((2, nz)),
            dma((2, steps)), dma((2, steps)), dma((2, steps)), dma((2, steps)),
        ],
        compiler_params=pltpu.CompilerParams(
            collective_id=0, has_side_effects=True, vmem_limit_bytes=58 * 1024 * 1024
        ),
    )(
        field.reshape(cells, ch), delta.reshape(cells, ch), mask.reshape(cells, ch),
        weight_one.reshape(3, wide, ch), bias_one.reshape(1, ch),
        weight_two.reshape(3, wide, ch), bias_two.reshape(1, ch), fold_partner,
    )
    scale = 1.0 / math.sqrt(cells * nz * nm)
    grads = sums.astype(F32) * scale
    shape = weight_one.shape
    return (
        out.reshape(field.shape), in_grad.reshape(field.shape),
        grads[0].reshape(shape), grads[1].reshape(shape),
    )


def solution(mesh):
    placed = (
        P("merid", "zonal", None), P(), P(), P(), P(), P("merid", "zonal"), P(),
        P("merid", "zonal", None),
    )
    return jax.shard_map(
        functools.partial(shards, nz=mesh.shape["zonal"], nm=mesh.shape["merid"]),
        mesh=mesh,
        in_specs=placed,
        out_specs=(P("merid", "zonal", None), P("merid", "zonal", None), P(), P()),
        check_vma=False,
    )
```

time: 437 us -> 94.5 us (0.22); the launches traced: 432 us -> 94.2 us
  blocking collectives: 102 us -> 0 us
  waiting for transfers between devices: 99.4 us -> 0 us
  Pallas kernels: 0 us -> 83.6 us
  local copies, waits for them, and re-layouts: 85.4 us -> 4.85 us
  starting transfers between devices: 57 us -> 0 us
  other arithmetic: 50.4 us -> 5.13 us
  matrix products: 23.1 us -> 0 us
  between operations: 15 us -> 0.67 us
    all_gather x4 -> x0, blocking collectives: 102 us -> none  [the longest x2 51.6 us: fold_forward(): whole_row = lax.all_gather(top_row, 'zonal', axis=0, tiled=True)]
    psum x1 -> x0, waiting for transfers between devices: 97.6 us -> none  [shards(): grad_one, grad_two = lax.psum((grad_one, grad_two), ('zonal', 'merid'))]
    pallas_call x0 -> x1, Pallas kernels: none -> 83.6 us  [shards(): pl.pallas_call(functools.partial(kernel, nz, nm, rows, cols, plans), out_...]
    ppermute x16 -> x0, starting transfers between devices: 56.9 us -> none  [the longest x8 48.8 us: with_halo(): lax.ppermute(head, axis, [((i + 1) % count, i) for i in range(ends)])]
    scatter-add x18 -> x0, local copies, waits for them, and re-layouts: 51.3 us -> none  [the longest x14 47.8 us: transpose_conv(): grad_pad.at[row_step:row_step + rows, col_step:col_step + columns]]
    dot_general x6 -> x0, matrix products: 23.1 us -> none  [the longest x2 10.3 us: kernel_grad(): lax.dot_general(patches, delta, (((0,), (0,)), ((), ())), preferred_eleme...]
    add x14 -> x0, other arithmetic: 21 us -> none  [the longest x10 19.7 us: transpose_conv(): grad_pad.at[row_step:row_step + rows, col_step:col_step + columns]]
    dot_general x2 -> x0, local copies, waits for them, and re-layouts: 13.4 us -> none  [kernel_grad(): lax.dot_general(patches, delta, (((0,), (0,)), ((), ())), preferred_eleme...]
  transfers between devices with their start and end apart: 17 -> 0, of which waited for: 3 -> 0; matrix products, arithmetic and copies ran while one was open for 27% -> 0% of each run, Pallas kernels for 0% -> 0%
where the time goes in v1:
time: 94.5 us; the launch traced here: 94.2 us
  Pallas kernels  83.6 us (88%)
  other arithmetic  5.13 us (5%)
  local copies, waits for them, and re-layouts  4.85 us (5%)
    pallas_call x1, Pallas kernels, shards(): pl.pallas_call(functools.partial(kernel, nz, nm, rows, cols, plans), out_...  83.6 us
    slice x1, local copies, waits for them, and re-layouts, shards(): grads[1].reshape(shape)  2.49 us
    mul x1, other arithmetic, shards(): grads = sums.astype(F32) * scale  2.08 us
    mul x1, other arithmetic, shards(): delta = cotangent * mask  2.04 us

profile of v1, /device:TPU:5, one launch (start us, length us, event | category | flops | bytes accessed | tf_op | source)
XLA Modules:
  0.0 94.2 jit_solution(9096550901547466019)
XLA Ops:
  0.6 0.8 lt.35
  1.4 1.0 %compare_convert_fusion.mask = bf16[1024,256]{1,0:T(8,128)(2,1)} fusion(s32[256]{0:T(256)S(1)} %and_select_fusion, s32[1024]{0:T(1024)S(1)} %lt.35), kind=kLoop, calls=%fused_computation.1 | loop fusion | flops 524288 | bytes 529408 | tf_op jit(solution)/shard_map/convert_element_type | solution.py:453
  2.4 2.0 %compare_select_fusion = bf16[16,64,256]{2,1,0:T(8,128)(2,1)} fusion(bf16[16,64,256]{2,1,0:T(8,128)(2,1)} %param.15, s32[16,64]{1,0:T(8,128)} %param.13, s32[256]{0:T(256)S(1)} %and_select_fusion), kind=kLoop, calls=%fused_computation.2 | loop fusion | flops 524288 | bytes 1053696 | tf_op jit(solution)/shard_map/mul | solution.py:454
  4.5 83.6 %shard_map.111 = (bf16[1024,256]{1,0:T(8,128)(2,1)}, bf16[1024,256]{1,0:T(8,128)(2,1)}, bf16[2,2304,256]{2,1,0:T(8,128)(2,1)}) custom-call(bf16[1024,256]{1,0:T(8,128)(2,1)} %bitcast.15, bf16[1024,256]{1,0:T(8,128)(2,1)} %bitcast.12, bf16[1024,256]{1,0:T(8,128)(2,1)} %compare_convert_fusion.mask, bf16[3,768,256]{2,1,0:T(8,128)(2,1)} %bitcast.13, ...), custom_call_target="tpu_custom_call" | custom-call | tf_op jit(solution)/shard_map/pallas_call | solution.py:463
  88.1 2.1 %convert_multiply_fusion = f32[2,2304,256]{2,1,0:T(8,128)S(1)} fusion(bf16[2,2304,256]{2,1,0:T(8,128)(2,1)} %get-tuple-element.9), kind=kLoop, calls=%fused_computation | loop fusion | flops 2359296 | bytes 7077888 | tf_op jit(solution)/shard_map/mul | solution.py:501
  90.1 0.0 copy-start.1
  90.2 0.0 copy-start
  90.2 2.5 %fusion = (f32[1,2304,256]{2,1,0:T(8,128)}, f32[1,2304,256]{2,1,0:T(8,128)}) fusion(f32[2,2304,256]{2,1,0:T(8,128)S(1)} %convert_multiply_fusion), kind=kLoop, calls=%fused_computation.4 | loop fusion | bytes 9437184 | tf_op jit(solution)/shard_map/slice | solution.py:505
  92.7 0.0 copy-done.1
  92.7 0.8 copy.14
  93.4 0.0 copy-done
  93.5 0.8 copy.15
  (1 shorter events, 0.0 us)
Async XLA Ops:
  90.1 2.5 %copy-start.1 = (bf16[1024,256]{1,0:T(8,128)(2,1)S(1)}, bf16[1024,256]{1,0:T(8,128)(2,1)}, u32[]{:S(2)}) copy-start(bf16[1024,256]{1,0:T(8,128)(2,1)} %get-tuple-element.7) | copy-start | bytes 1572868
  90.2 3.3 %copy-start = (bf16[1024,256]{1,0:T(8,128)(2,1)S(1)}, bf16[1024,256]{1,0:T(8,128)(2,1)}, u32[]{:S(2)}) copy-start(bf16[1024,256]{1,0:T(8,128)(2,1)} %get-tuple-element.8) | copy-start | bytes 1572868

commit v2 on v1

--- a/solution.py
+++ b/solution.py
@@ -19,11 +19,11 @@
 def plan_steps(total, nz, nm):
     merid_bits = [("merid", 1 << i) for i in range(nm.bit_length() - 1)]
     zonal_bits = [("zonal", 1 << i) for i in range(nz.bit_length() - 1)]
-    order_one = merid_bits + zonal_bits
-    order_two = merid_bits[:1] + zonal_bits[1:2] + merid_bits[1:] + zonal_bits[:1] + zonal_bits[2:]
+    rest = merid_bits[1:] + zonal_bits
     plans = []
-    for order in (order_one, order_two):
-        size, plan = total, []
+    for turn in range(3):
+        order = merid_bits[:1] + rest[turn:3] + rest[:turn] + rest[3:]
+        size, plan = total // 3, []
         for step, (axis, bit) in enumerate(order):
             halve = size % 32 == 0
             if halve:
@@ -267,14 +267,13 @@
     def last_row(ql, wl, target):
         target[cells - cols:, :] += jnp.dot(ql[...], wl[...], preferred_element_type=F32)
 
-    def gradient(g, q, e_turned):
-        for a in range(3):
-            for b in range(3):
-                part = jnp.dot(
-                    e_turned, q[a * cols:a * cols + cells, b * ch:(b + 1) * ch],
-                    preferred_element_type=F32,
-                )
-                acc[g, (3 * a + b) * ch:(3 * a + b + 1) * ch, :] = part.T
+    def gradient(g, a, q, e_turned):
+        for b in range(3):
+            part = jnp.dot(
+                e_turned, q[a * cols:a * cols + cells, b * ch:(b + 1) * ch],
+                preferred_element_type=F32,
+            )
+            acc[g, (3 * a + b) * ch:(3 * a + b + 1) * ch, :] = part.T
 
     def loop_rows(count, body):
         piece = 48 if count % 48 == 0 else 16
@@ -283,13 +282,15 @@
         def _(i):
             body(i * piece, piece)
 
-    def reduce_all(g):
-        low = 0
+    def reduce_all(g, a):
+        lane = 3 * g + a
+        plan = plans[a]
+        low = 3 * a * ch
         place = 0
         place_wide = 0
         waits = []
         gathers = []
-        for step, (axis, bit, size, halve, wide) in enumerate(plans[g]):
+        for step, (axis, bit, size, halve, wide) in enumerate(plan):
             mine, other = partner_of(axis, bit)
             keep = low + mine * size if halve else low
             give = low + (1 - mine) * size if halve else low
@@ -297,7 +298,7 @@
                 gathers.append((step, axis, bit, size, low))
 
             def fill(off, piece, give=give, place=place):
-                ar_send[g, pl.ds(place + pl.multiple_of(off, 16), piece), :] = acc[
+                ar_send[lane, pl.ds(place + pl.multiple_of(off, 16), piece), :] = acc[
                     g, pl.ds(pl.multiple_of(give + off, 16), piece), :
                 ].astype(BF)
 
@@ -307,11 +308,11 @@
                 place_wide += size
             else:
                 loop_rows(size, fill)
-                source = ar_send.at[g, pl.ds(place, size)]
+                source = ar_send.at[lane, pl.ds(place, size)]
                 landing, start = ar_recv, place
             copy = copy_to(
-                source, landing.at[g, pl.ds(start, size)],
-                ar_ss.at[g, step], ar_rs.at[g, step], other["merid"], other["zonal"],
+                source, landing.at[lane, pl.ds(start, size)],
+                ar_ss.at[lane, step], ar_rs.at[lane, step], other["merid"], other["zonal"],
             )
             copy.start()
             yield
@@ -327,14 +328,14 @@
             ):
                 at = pl.ds(pl.multiple_of(keep + off, 16), piece)
                 here = pl.ds(start + pl.multiple_of(off, 16), piece)
-                own = ar_send[g, here, :].astype(F32) if rounded else acc[g, at, :]
-                acc[g, at, :] = own + landing[g, here, :].astype(F32)
+                own = ar_send[lane, here, :].astype(F32) if rounded else acc[g, at, :]
+                acc[g, at, :] = own + landing[lane, here, :].astype(F32)
 
             loop_rows(size, add)
             if not wide:
                 place += size
             low = keep
-        final = plans[g][-1][2]
+        final = plan[-1][2]
 
         def settle(off, piece, low=low):
             at = pl.ds(pl.multiple_of(low + off, 16), piece)
@@ -347,14 +348,14 @@
             at = pl.ds(pl.multiple_of(base + mine * size, 16), size)
             theirs = pl.ds(pl.multiple_of(base + (1 - mine) * size, 16), size)
             copy = copy_to(
-                sums.at[g, at], sums.at[g, at], ag_ss.at[g, step], ag_rs.at[g, step],
+                sums.at[g, at], sums.at[g, at], ag_ss.at[lane, step], ag_rs.at[lane, step],
                 other["merid"], other["zonal"],
             )
             copy.start()
             waits.append(copy)
             yield
             copy_to(
-                sums.at[g, theirs], sums.at[g, theirs], ag_ss.at[g, step], ag_rs.at[g, step],
+                sums.at[g, theirs], sums.at[g, theirs], ag_ss.at[lane, step], ag_rs.at[lane, step],
                 other["merid"], other["zonal"],
             ).wait_recv()
         for copy in waits:
@@ -401,43 +402,49 @@
     prepare(1)
     halo(1, "start")
 
-    gradient(0, q_field, vb[...].T.astype(BF))
-    first = reduce_all(0)
-    next(first)
+    chains = []
+
+    def advance():
+        going = [next(chain, "end") != "end" for chain in chains]
+        return any(going)
+
+    def begin(g, a, q, e_turned):
+        gradient(g, a, q, e_turned)
+        chain = reduce_all(g, a)
+        next(chain)
+        chains.append(chain)
+
+    turned = vb[...].T.astype(BF)
+    for a in range(3):
+        begin(0, a, q_field, turned)
     halo_arrive(1)
     assemble(1, 0, va, q_hidden, None)
+    advance()
+    turned = delta_in[...].astype(F32).T.astype(BF)
+    for a in range(3):
+        begin(1, a, q_hidden, turned)
+    advance()
+
     assemble(1, 1, vb, q_one, ql_one)
-    next(first)
-    gradient(1, q_hidden, delta_in[...].astype(F32).T.astype(BF))
-    second = reduce_all(1)
-    next(second)
-
-    def advance(gen):
-        return next(gen, "end") != "end"
-
-    advance(first)
-    advance(second)
+    advance()
 
     def finish_out(at, total):
         full = field[at, :].astype(F32) + total + b_two[...]
         out[at, :] = (full * mask[at, :].astype(F32)).astype(BF)
 
     conv(q_hidden, w_two, finish_out)
-    advance(first)
-    advance(second)
+    advance()
     conv(q_one, wt_one, finish_hg)
     last_row(ql_one, wl_one, hg)
+    advance()
 
     @pl.loop(0, rows)
     def _(y):
         at = pl.ds(pl.multiple_of(y * cols, cols), cols)
         in_grad[at, :] = (delta_in[at, :].astype(F32) + hg[at, :]).astype(BF)
 
-    more = True
-    while more:
-        one = advance(first)
-        two = advance(second)
-        more = one or two
+    while advance():
+        pass
     halo(0, "wait_send")
     halo(1, "wait_send")
 
@@ -484,10 +491,10 @@
             pltpu.VMEM((2, 2, 2 * cols, ch), BF), pltpu.VMEM((2, 6, 2 * rows, ch), BF),
             pltpu.VMEM((2, nz, 2 * cols, ch), BF),
             pltpu.VMEM((2, total, ch), F32),
-            pltpu.VMEM((2, sent, ch), BF), pltpu.VMEM((2, sent, ch), BF),
-            pltpu.VMEM((2, sent_wide, ch), F32),
+            pltpu.VMEM((6, sent, ch), BF), pltpu.VMEM((6, sent, ch), BF),
+            pltpu.VMEM((6, sent_wide, ch), F32),
             dma((2, 8)), dma((2, 8)), dma((2, nz)), dma((2, nz)),
-            dma((2, steps)), dma((2, steps)), dma((2, steps)), dma((2, steps)),
+            dma((6, steps)), dma((6, steps)), dma((6, steps)), dma((6, steps)),
         ],
         compiler_params=pltpu.CompilerParams(
             collective_id=0, has_side_effects=True, vmem_limit_bytes=58 * 1024 * 1024

time: 94.5 us -> 79.9 us (0.85)
  Pallas kernels: 83.6 us -> 68.4 us
    pallas_call x1, Pallas kernels: 83.6 us -> 68.4 us  [shards(): pl.pallas_call(functools.partial(kernel, nz, nm, rows, cols, plans), out_...]
where the time goes in v2:
time: 79.9 us; the launch traced here: 79 us
  Pallas kernels  68.4 us (86%)
  other arithmetic  5.13 us (6%)
  local copies, waits for them, and re-layouts  4.85 us (6%)
    pallas_call x1, Pallas kernels, shards(): pl.pallas_call(functools.partial(kernel, nz, nm, rows, cols, plans), out_...  68.4 us
    slice x1, local copies, waits for them, and re-layouts, shards(): grads[1].reshape(shape)  2.49 us
    mul x1, other arithmetic, shards(): grads = sums.astype(F32) * scale  2.08 us
    mul x1, other arithmetic, shards(): delta = cotangent * mask  2.04 us

profile of v2, /device:TPU:5, one launch (start us, length us, event | category | flops | bytes accessed | tf_op | source)
XLA Modules:
  0.0 79.0 jit_solution(6299553675306557008)
XLA Ops:
  0.6 0.8 lt.35
  1.4 1.0 %compare_convert_fusion.mask = bf16[1024,256]{1,0:T(8,128)(2,1)} fusion(s32[256]{0:T(256)S(1)} %and_select_fusion, s32[1024]{0:T(1024)S(1)} %lt.35), kind=kLoop, calls=%fused_computation.1 | loop fusion | flops 524288 | bytes 529408 | tf_op jit(solution)/shard_map/convert_element_type | solution.py:460
  2.4 2.0 %compare_select_fusion = bf16[16,64,256]{2,1,0:T(8,128)(2,1)} fusion(bf16[16,64,256]{2,1,0:T(8,128)(2,1)} %param.15, s32[16,64]{1,0:T(8,128)} %param.13, s32[256]{0:T(256)S(1)} %and_select_fusion), kind=kLoop, calls=%fused_computation.2 | loop fusion | flops 524288 | bytes 1053696 | tf_op jit(solution)/shard_map/mul | solution.py:461
  4.5 68.4 %shard_map.111 = (bf16[1024,256]{1,0:T(8,128)(2,1)}, bf16[1024,256]{1,0:T(8,128)(2,1)}, bf16[2,2304,256]{2,1,0:T(8,128)(2,1)}) custom-call(bf16[1024,256]{1,0:T(8,128)(2,1)} %bitcast.15, bf16[1024,256]{1,0:T(8,128)(2,1)} %bitcast.12, bf16[1024,256]{1,0:T(8,128)(2,1)} %compare_convert_fusion.mask, bf16[3,768,256]{2,1,0:T(8,128)(2,1)} %bitcast.13, ...), custom_call_target="tpu_custom_call" | custom-call | tf_op jit(solution)/shard_map/pallas_call | solution.py:470
  72.8 2.1 %convert_multiply_fusion = f32[2,2304,256]{2,1,0:T(8,128)S(1)} fusion(bf16[2,2304,256]{2,1,0:T(8,128)(2,1)} %get-tuple-element.9), kind=kLoop, calls=%fused_computation | loop fusion | flops 2359296 | bytes 7077888 | tf_op jit(solution)/shard_map/mul | solution.py:508
  74.9 0.0 copy-start.1
  74.9 0.0 copy-start
  74.9 2.5 %fusion = (f32[1,2304,256]{2,1,0:T(8,128)}, f32[1,2304,256]{2,1,0:T(8,128)}) fusion(f32[2,2304,256]{2,1,0:T(8,128)S(1)} %convert_multiply_fusion), kind=kLoop, calls=%fused_computation.4 | loop fusion | bytes 9437184 | tf_op jit(solution)/shard_map/slice | solution.py:512
  77.4 0.0 copy-done.1
  77.4 0.8 %copy.14 = bf16[16,64,256]{2,1,0:T(8,128)(2,1)} copy(bf16[16,64,256]{2,1,0:T(8,128)(2,1)S(1)} %bitcast.17) | data formatting | bytes 1048576
  78.2 0.0 copy-done
  78.2 0.8 %copy.15 = bf16[16,64,256]{2,1,0:T(8,128)(2,1)} copy(bf16[16,64,256]{2,1,0:T(8,128)(2,1)S(1)} %bitcast.16) | data formatting | bytes 1048576
  (1 shorter events, 0.0 us)
Async XLA Ops:
  74.9 2.5 %copy-start.1 = (bf16[1024,256]{1,0:T(8,128)(2,1)S(1)}, bf16[1024,256]{1,0:T(8,128)(2,1)}, u32[]{:S(2)}) copy-start(bf16[1024,256]{1,0:T(8,128)(2,1)} %get-tuple-element.7) | copy-start | bytes 1572868
  74.9 3.3 %copy-start = (bf16[1024,256]{1,0:T(8,128)(2,1)S(1)}, bf16[1024,256]{1,0:T(8,128)(2,1)}, u32[]{:S(2)}) copy-start(bf16[1024,256]{1,0:T(8,128)(2,1)} %get-tuple-element.8) | copy-start | bytes 1572868

commit v3 on v2

--- a/solution.py
+++ b/solution.py
@@ -35,9 +35,9 @@
 
 def kernel(
     nz, nm, rows, cols, plans,
-    field, delta_in, mask, w_one, b_one, w_two, b_two, partner_tab,
+    field, cotangent, depth, w_one, b_one, w_two, b_two, partner_tab,
     out, in_grad, sums,
-    va, vb, gp, hg,
+    va, vb, gp, hg, mask, delta_in,
     q_field, q_hidden, q_two, q_one, ql_two, ql_one, wt_one, wt_two, wl_one, wl_two,
     west, east, north, south, cols32,
     row_send, col_send, row_recv, col_recv, fold_all, acc, ar_send, ar_recv, ar_wide,
@@ -221,7 +221,7 @@
             west[rows + 1:rows + 2, :] = folded[cols:cols + 1, :]
             east[rows + 1:rows + 2, :] = folded[cols + 1:cols + 2, :]
 
-        @pl.loop(0, rows)
+        @pl.loop(0, rows, unroll=2)
         def _(y):
             off = pl.multiple_of(y * cols, cols)
             emit(
@@ -276,7 +276,7 @@
             acc[g, (3 * a + b) * ch:(3 * a + b + 1) * ch, :] = part.T
 
     def loop_rows(count, body):
-        piece = 48 if count % 48 == 0 else 16
+        piece = next(size for size in (192, 96, 48, 16) if count % size == 0)
 
         @pl.loop(0, count // piece)
         def _(i):
@@ -362,7 +362,17 @@
             copy.wait_send()
 
     va[...] = field[...].astype(F32)
-    vb[...] = delta_in[...].astype(F32)
+    channel = lax.broadcasted_iota(jnp.int32, (cols, ch), 1)
+    level = channel
+    for first in range(LEV, ch, LEV):
+        level = level - jnp.where(channel >= first, LEV, 0)
+    for y in range(rows):
+        at = slice(y * cols, (y + 1) * cols)
+        wet = jnp.where(level < depth[:, y:y + 1], 1.0, 0.0)
+        masked = cotangent[at, :].astype(F32) * wet
+        mask[at, :] = wet
+        vb[at, :] = masked
+        delta_in[at, :] = masked.astype(BF)
     prepare(0)
     count = (
         2 + len(plans[0]) + jnp.where(has_n, 3, 0) + jnp.where(has_s, 3, 0)
@@ -378,7 +388,7 @@
 
     def finish_one(at, total):
         x = total + b_one[...]
-        keep = mask[at, :].astype(F32)
+        keep = mask[at, :]
         square = x * x
         t = jnp.tanh(GELU_A * x * (1.0 + GELU_B * square))
         half = 0.5 * (1.0 + t)
@@ -430,7 +440,7 @@
 
     def finish_out(at, total):
         full = field[at, :].astype(F32) + total + b_two[...]
-        out[at, :] = (full * mask[at, :].astype(F32)).astype(BF)
+        out[at, :] = (full * mask[at, :]).astype(BF)
 
     conv(q_hidden, w_two, finish_out)
     advance()
@@ -456,9 +466,6 @@
     rows, cols, ch = field.shape
     cells = rows * cols
     total = 9 * ch
-    level = lax.broadcasted_iota(jnp.int32, (1, 1, ch), 2) % LEV
-    mask = (level < depth_levels[:, :, None]).astype(BF)
-    delta = cotangent * mask
     plans = plan_steps(total, nz, nm)
     sent = max(sum(step[2] for step in plan if not step[4]) for plan in plans)
     sent_wide = max(sum(step[2] for step in plan if step[4]) for plan in plans)
@@ -479,6 +486,7 @@
         scratch_shapes=[
             pltpu.VMEM((cells, ch), F32), pltpu.VMEM((cells, ch), F32),
             pltpu.VMEM((cells, ch), F32), pltpu.VMEM((cells, ch), F32),
+            pltpu.VMEM((cells, ch), F32), pltpu.VMEM((cells, ch), BF),
             pltpu.VMEM((cells + 2 * cols, wide), BF), pltpu.VMEM((cells + 2 * cols, wide), BF),
             pltpu.VMEM((cells + 2 * cols, wide), BF), pltpu.VMEM((cells + 2 * cols, wide), BF),
             pltpu.VMEM((cols, wide), BF), pltpu.VMEM((cols, wide), BF),
@@ -500,7 +508,7 @@
             collective_id=0, has_side_effects=True, vmem_limit_bytes=58 * 1024 * 1024
         ),
     )(
-        field.reshape(cells, ch), delta.reshape(cells, ch), mask.reshape(cells, ch),
+        field.reshape(cells, ch), cotangent.reshape(cells, ch), depth_levels.T,
         weight_one.reshape(3, wide, ch), bias_one.reshape(1, ch),
         weight_two.reshape(3, wide, ch), bias_two.reshape(1, ch), fold_partner,
     )

time: 79.9 us -> 77.6 us (0.971)
  other arithmetic: 5.13 us -> 2.08 us
    mul x1 -> x0, other arithmetic: 2.04 us -> none  [shards(): delta = cotangent * mask]
    unnamed x6 -> x7, local copies, waits for them, and re-layouts: 1.59 us -> 2.99 us
    convert_element_type x1 -> x0, other arithmetic: 1 us -> none  [shards(): mask = (level < depth_levels[:, :, None]).astype(BF)]
where the time goes in v3:
time: 77.6 us; the launch traced here: 76.5 us
  Pallas kernels  68.3 us (88%)
  local copies, waits for them, and re-layouts  5.48 us (7%)
  other arithmetic  2.08 us (3%)
    pallas_call x1, Pallas kernels, shards(): pl.pallas_call(functools.partial(kernel, nz, nm, rows, cols, plans), out_...  68.3 us
    unnamed x7, local copies, waits for them, and re-layouts  2.99 us
    slice x1, local copies, waits for them, and re-layouts, shards(): grads[1].reshape(shape)  2.49 us
    mul x1, other arithmetic, shards(): grads = sums.astype(F32) * scale  2.08 us

profile of v3, /device:TPU:5, one launch (start us, length us, event | category | flops | bytes accessed | tf_op | source)
XLA Modules:
  0.0 76.5 jit_solution(18294068713158362281)
XLA Ops:
  0.6 1.4 %copy.12 = s32[16,64]{0,1:T(8,128)} copy(s32[16,64]{1,0:T(8,128)} %param.13) | data formatting | bytes 8192 | tf_op args[5]
  2.0 68.3 %shard_map.111 = (bf16[1024,256]{1,0:T(8,128)(2,1)}, bf16[1024,256]{1,0:T(8,128)(2,1)}, bf16[2,2304,256]{2,1,0:T(8,128)(2,1)}) custom-call(bf16[1024,256]{1,0:T(8,128)(2,1)} %bitcast.17, bf16[1024,256]{1,0:T(8,128)(2,1)} %bitcast.18, s32[64,16]{1,0:T(8,128)} %bitcast.19, bf16[3,768,256]{2,1,0:T(8,128)(2,1)} %bitcast.13, f32[1,256]{1,0:T(1,128)} %bitcast.20, ...), custom_call_target="tpu_custom_call" | custom-call | tf_op jit(solution)/shard_map/pallas_call | solution.py:477
  70.3 2.1 %convert_multiply_fusion = f32[2,2304,256]{2,1,0:T(8,128)S(1)} fusion(bf16[2,2304,256]{2,1,0:T(8,128)(2,1)} %get-tuple-element.9), kind=kLoop, calls=%fused_computation | loop fusion | flops 2359296 | bytes 7077888 | tf_op jit(solution)/shard_map/mul | solution.py:516
  72.4 0.0 copy-start.1
  72.4 0.0 copy-start
  72.4 2.5 %fusion = (f32[1,2304,256]{2,1,0:T(8,128)}, f32[1,2304,256]{2,1,0:T(8,128)}) fusion(f32[2,2304,256]{2,1,0:T(8,128)S(1)} %convert_multiply_fusion), kind=kLoop, calls=%fused_computation.1 | loop fusion | bytes 9437184 | tf_op jit(solution)/shard_map/slice | solution.py:520
  74.9 0.0 copy-done.1
  74.9 0.8 %copy.15 = bf16[16,64,256]{2,1,0:T(8,128)(2,1)} copy(bf16[16,64,256]{2,1,0:T(8,128)(2,1)S(1)} %bitcast.16) | data formatting | bytes 1048576
  75.7 0.0 copy-done
  75.7 0.8 %copy.16 = bf16[16,64,256]{2,1,0:T(8,128)(2,1)} copy(bf16[16,64,256]{2,1,0:T(8,128)(2,1)S(1)} %bitcast.15) | data formatting | bytes 1048576
Async XLA Ops:
  72.4 2.5 %copy-start.1 = (bf16[1024,256]{1,0:T(8,128)(2,1)S(1)}, bf16[1024,256]{1,0:T(8,128)(2,1)}, u32[]{:S(2)}) copy-start(bf16[1024,256]{1,0:T(8,128)(2,1)} %get-tuple-element.7) | copy-start | bytes 1572868
  72.4 3.3 %copy-start = (bf16[1024,256]{1,0:T(8,128)(2,1)S(1)}, bf16[1024,256]{1,0:T(8,128)(2,1)}, u32[]{:S(2)}) copy-start(bf16[1024,256]{1,0:T(8,128)(2,1)} %get-tuple-element.8) | copy-start | bytes 1572868

commit v4 on v3

--- a/solution.py
+++ b/solution.py
@@ -381,7 +381,6 @@
     pl.semaphore_wait(barrier, count)
     halo(0, "start")
     transpose_weights(w_two, wt_two, wl_two)
-    transpose_weights(w_one, wt_one, wl_one)
     halo_arrive(0)
     assemble(0, 0, va, q_field, None)
     assemble(0, 1, vb, q_two, ql_two)
@@ -443,6 +442,8 @@
         out[at, :] = (full * mask[at, :]).astype(BF)
 
     conv(q_hidden, w_two, finish_out)
+    advance()
+    transpose_weights(w_one, wt_one, wl_one)
     advance()
     conv(q_one, wt_one, finish_hg)
     last_row(ql_one, wl_one, hg)

time: 77.6 us -> 77.5 us (level)
  no operation moved by 1% of the time
where the time goes in v4:
time: 77.5 us; the launch traced here: 76.7 us
  Pallas kernels  68.4 us (88%)
  local copies, waits for them, and re-layouts  5.48 us (7%)
  other arithmetic  2.08 us (3%)
    pallas_call x1, Pallas kernels, shards(): pl.pallas_call(functools.partial(kernel, nz, nm, rows, cols, plans), out_...  68.4 us
    unnamed x7, local copies, waits for them, and re-layouts  2.99 us
    slice x1, local copies, waits for them, and re-layouts, shards(): grads[1].reshape(shape)  2.49 us
    mul x1, other arithmetic, shards(): grads = sums.astype(F32) * scale  2.08 us

profile of v4, /device:TPU:5, one launch (start us, length us, event | category | flops | bytes accessed | tf_op | source)
XLA Modules:
  0.0 76.7 jit_solution(4569247641364003050)
XLA Ops:
  0.6 1.4 %copy.12 = s32[16,64]{0,1:T(8,128)} copy(s32[16,64]{1,0:T(8,128)} %param.13) | data formatting | bytes 8192 | tf_op args[5]
  2.0 68.4 %shard_map.111 = (bf16[1024,256]{1,0:T(8,128)(2,1)}, bf16[1024,256]{1,0:T(8,128)(2,1)}, bf16[2,2304,256]{2,1,0:T(8,128)(2,1)}) custom-call(bf16[1024,256]{1,0:T(8,128)(2,1)} %bitcast.17, bf16[1024,256]{1,0:T(8,128)(2,1)} %bitcast.18, s32[64,16]{1,0:T(8,128)} %bitcast.19, bf16[3,768,256]{2,1,0:T(8,128)(2,1)} %bitcast.13, f32[1,256]{1,0:T(1,128)} %bitcast.20, ...), custom_call_target="tpu_custom_call" | custom-call | tf_op jit(solution)/shard_map/pallas_call | solution.py:478
  70.5 2.1 %convert_multiply_fusion = f32[2,2304,256]{2,1,0:T(8,128)S(1)} fusion(bf16[2,2304,256]{2,1,0:T(8,128)(2,1)} %get-tuple-element.9), kind=kLoop, calls=%fused_computation | loop fusion | flops 2359296 | bytes 7077888 | tf_op jit(solution)/shard_map/mul | solution.py:517
  72.6 0.0 copy-start.1
  72.6 0.0 copy-start
  72.6 2.5 %fusion = (f32[1,2304,256]{2,1,0:T(8,128)}, f32[1,2304,256]{2,1,0:T(8,128)}) fusion(f32[2,2304,256]{2,1,0:T(8,128)S(1)} %convert_multiply_fusion), kind=kLoop, calls=%fused_computation.1 | loop fusion | bytes 9437184 | tf_op jit(solution)/shard_map/slice | solution.py:521
  75.1 0.0 copy-done.1
  75.1 0.8 %copy.15 = bf16[16,64,256]{2,1,0:T(8,128)(2,1)} copy(bf16[16,64,256]{2,1,0:T(8,128)(2,1)S(1)} %bitcast.16) | data formatting | bytes 1048576
  75.9 0.0 copy-done
  75.9 0.8 %copy.16 = bf16[16,64,256]{2,1,0:T(8,128)(2,1)} copy(bf16[16,64,256]{2,1,0:T(8,128)(2,1)S(1)} %bitcast.15) | data formatting | bytes 1048576
Async XLA Ops:
  72.6 2.5 %copy-start.1 = (bf16[1024,256]{1,0:T(8,128)(2,1)S(1)}, bf16[1024,256]{1,0:T(8,128)(2,1)}, u32[]{:S(2)}) copy-start(bf16[1024,256]{1,0:T(8,128)(2,1)} %get-tuple-element.7) | copy-start | bytes 1572868
  72.6 3.3 %copy-start = (bf16[1024,256]{1,0:T(8,128)(2,1)S(1)}, bf16[1024,256]{1,0:T(8,128)(2,1)}, u32[]{:S(2)}) copy-start(bf16[1024,256]{1,0:T(8,128)(2,1)} %get-tuple-element.8) | copy-start | bytes 1572868
